TPU v7x, 128 devices: a whole 4x4x4 slice. The times are simulated.
128 devices in a mesh: dom: 8 (over z, core), grp: 16 (over x, y).
Axes of the slice: x: 4, y: 4, z: 4, core: 2. Of those that a mesh axis runs over, the one named last changes fastest.
Arguments:
- inputs: bfloat16 [393216, 256], P(('dom', 'grp')), may hold values from -6 to 6
- initial: bfloat16 [393216, 256], P(('dom', 'grp')), may hold values from -6 to 6
- history: bfloat16 [393216, 256], P(('dom', 'grp')), may hold values from -6 to 6
- upstream: bfloat16 [393216, 256], P(('dom', 'grp')), may hold values from -6 to 6
- weight: bfloat16 [256, 256], replicated, may hold values from -0.375 to 0.375
- tile_vals: bfloat16 [36864, 128, 128], P(('dom', 'grp')), may hold values from 0 to 0.088378906
- tile_row: int32 [36864], P(('dom', 'grp')), may hold values from 0 to 23
- tile_col: int32 [36864], P(('dom', 'grp')), may hold values from 0 to 47, as said below
- tile_count: int32 [128], P(('dom', 'grp')), may hold values from 48 to 288, as said below
- send_rows: int32 [8, 16, 128, 8], P('dom', 'grp'), may hold values from 0 to 3071
- cache_ask: int32 [8, 16, 8, 2], P('dom', 'grp'), may hold values from 0 to 23
Outputs:
- layer_out: bfloat16 [393216, 256], P(('dom', 'grp'))
- grad_inputs: float32 [393216, 256], P(('dom', 'grp'))
- grad_weight: float32 [256, 256], replicated
Inputs may be any that keep to these rules, and one draw needn't show every extreme that they name: `send_rows`: row numbers within the sending section. `cache_ask`: block numbers within the owning section. `tile_row`: row block within the section. `tile_col`: in each section's list the first 48 tiles name every column block once. `tile_count`: some section has exactly 288 live tiles.
All inputs are finite; a program needn't handle non-finite values.
Results may differ from a plain program's by a relative error of at most 0.0053.
Values may be sent and summed in bfloat16 or wider, within the bound.
A program may use at most 128 MiB of HBM per device.

v0:
```python
import math
import jax
import jax.numpy as jnp
from jax import lax
from jax.sharding import PartitionSpec as P

alpha_res = 0.1
beta_map = 0.4


def silu_slope(pre_act):
    squash = jax.nn.sigmoid(pre_act)
    return squash * (1.0 + pre_act * (1.0 - squash))


def turn_width(slot_count):
    for option_width in (96, 48, 32, 16, 8):
        return option_width
    return slot_count


def per_device(
    inputs,
    initial,
    history,
    upstream,
    weight,
    tile_vals,
    tile_row,
    tile_col,
    tile_count,
    send_rows,
    cache_ask,
):
    row_count, feature_dim = inputs.shape
    block_rows = tile_vals.shape[1]
    block_count = row_count // block_rows
    slot_count = tile_vals.shape[0]
    group_size = turn_width(slot_count)
    dom_count = lax.axis_size("dom")
    grp_count = lax.axis_size("grp")
    peer_count = dom_count * grp_count
    send_list = send_rows.reshape(peer_count, -1)
    per_peer = send_list.shape[1]
    ask_list = cache_ask.reshape(dom_count, -1)
    asked_per = ask_list.shape[1]
    outgoing = inputs[send_list.reshape(-1)].reshape(peer_count, per_peer, feature_dim)
    arrived = lax.all_to_all(outgoing, ("dom", "grp"), split_axis=0, concat_axis=0, tiled=True)
    arrived = arrived.reshape(peer_count * per_peer, feature_dim)
    wanted = lax.all_to_all(ask_list, "dom", split_axis=0, concat_axis=0, tiled=True)
    own_blocks = history.reshape(block_count, block_rows, feature_dim)
    served = own_blocks[wanted.reshape(-1)].reshape(dom_count, asked_per * block_rows, feature_dim)
    cached = lax.all_to_all(served, "dom", split_axis=0, concat_axis=0, tiled=True)
    cached = cached.reshape(dom_count * asked_per * block_rows, feature_dim)
    columns = jnp.concatenate([inputs, arrived, cached], axis=0)
    col_blocks = columns.reshape(-1, block_rows, feature_dim)
    column_total = col_blocks.shape[0]
    live_count = tile_count[0]
    turn_count = (live_count + group_size - 1) // group_size

    def turn_slices(turn_index):
        offset = turn_index * group_size
        tile_block = lax.dynamic_slice_in_dim(tile_vals, offset, group_size, 0)
        row_pick = lax.dynamic_slice_in_dim(tile_row, offset, group_size, 0)
        col_pick = lax.dynamic_slice_in_dim(tile_col, offset, group_size, 0)
        live_part = (offset + jnp.arange(group_size) < live_count).astype(jnp.float32)
        return (tile_block, row_pick, col_pick, live_part)

    def forward_turn(turn_index, totals):
        tile_block, row_pick, col_pick, live_part = turn_slices(turn_index)
        products = jnp.einsum(
            "tij,tjd->tid", tile_block, col_blocks[col_pick], preferred_element_type=jnp.float32
        )
        placing = (row_pick[:, None] == jnp.arange(block_count)[None, :]).astype(
            jnp.float32
        ) * live_part[:, None]
        return totals + jnp.einsum(
            "tr,tid->rid", placing, products, precision=lax.Precision.HIGHEST
        )

    gathered = lax.fori_loop(
        0, turn_count, forward_turn, jnp.zeros((block_count, block_rows, feature_dim), jnp.float32)
    )
    mixture = (1.0 - alpha_res) * gathered.reshape(
        row_count, feature_dim
    ) + alpha_res * initial.astype(jnp.float32)
    mixed_b = mixture.astype(jnp.bfloat16)
    pre_act = (1.0 - beta_map) * mixture + beta_map * jnp.dot(
        mixed_b, weight, preferred_element_type=jnp.float32
    )
    layer_out = jax.nn.silu(pre_act).astype(jnp.bfloat16)
    act_slope = upstream.astype(jnp.float32) * silu_slope(pre_act)
    slope_b = act_slope.astype(jnp.bfloat16)
    weight_part = lax.dot_general(
        mixed_b, slope_b, (((0,), (0,)), ((), ())), preferred_element_type=jnp.float32
    )
    through_weight = lax.dot_general(
        slope_b, weight, (((1,), (1,)), ((), ())), preferred_element_type=jnp.float32
    )
    back_grad = (
        (1.0 - alpha_res) * ((1.0 - beta_map) * act_slope + beta_map * through_weight)
    ).astype(jnp.bfloat16)
    back_blocks = back_grad.reshape(block_count, block_rows, feature_dim)

    def backward_turn(turn_index, totals):
        tile_block, row_pick, col_pick, live_part = turn_slices(turn_index)
        spread = jnp.einsum(
            "tji,tjd->tid", tile_block, back_blocks[row_pick], preferred_element_type=jnp.float32
        )
        onto_mask = (col_pick[:, None] == jnp.arange(column_total)[None, :]).astype(
            jnp.float32
        ) * live_part[:, None]
        return totals + jnp.einsum(
            "tc,tid->cid", onto_mask, spread, precision=lax.Precision.HIGHEST
        )

    column_grads = lax.fori_loop(
        0,
        turn_count,
        backward_turn,
        jnp.zeros((column_total, block_rows, feature_dim), jnp.float32),
    )
    fresh_blocks = peer_count * per_peer // block_rows
    own_grads = column_grads[:block_count].reshape(row_count, feature_dim)
    fresh_grads = (
        column_grads[block_count : block_count + fresh_blocks]
        .reshape(peer_count, per_peer, feature_dim)
        .astype(jnp.bfloat16)
    )
    returned = lax.all_to_all(fresh_grads, ("dom", "grp"), split_axis=0, concat_axis=0, tiled=True)
    returned = returned.reshape(peer_count * per_peer, feature_dim).astype(jnp.float32)
    grad_inputs = own_grads.at[send_list.reshape(-1)].add(returned)
    weight_total = lax.psum(weight_part, ("dom", "grp"))
    grad_weight = weight_total * (beta_map / math.sqrt(row_count * peer_count))
    return (layer_out, grad_inputs, grad_weight)


def solution(mesh):
    placed = (
        P(("dom", "grp"), None),
        P(("dom", "grp"), None),
        P(("dom", "grp"), None),
        P(("dom", "grp"), None),
        P(),
        P(("dom", "grp"), None, None),
        P(("dom", "grp")),
        P(("dom", "grp")),
        P(("dom", "grp")),
        P("dom", "grp", None, None),
        P("dom", "grp", None, None),
    )
    return jax.shard_map(
        per_device,
        mesh=mesh,
        in_specs=placed,
        out_specs=(P(("dom", "grp"), None), P(("dom", "grp"), None), P()),
        check_vma=False,
    )
```

profile of v0, /device:TPU:1, one launch (start us, length us, event | category | flops | bytes accessed | tf_op | source)
XLA Modules:
  0.0 450.1 jit_solution(1641534458222594287)
XLA Ops:
  8.6 6.8 %all-to-all-start.1 = ((s32[8,1,2]{2,1,0:T(1,128)}), s32[8,1,2]{2,1,0:T(1,128)S(1)}, u32[]{:S(2)}, u32[]{:S(2)}) async-start(s32[8,1,2]{2,1,0:T(1,128)} %copy.25), calls=%async_computation.1 | async-start | bytes 8192 | tf_op jit(solution)/shard_map/all_to_all | solution.py:50
  17.0 6.2 %gather_fusion.2 = bf16[1024,256]{1,0:T(8,128)(2,1)} fusion(bf16[3072,256]{1,0:T(8,128)(2,1)} %param.15, s32[1024]{0:T(1024)S(1)} %broadcast_clamp_fusion), kind=kCustom, calls=%fused_computation.2 | custom fusion | bytes 1052672 | tf_op jit(solution)/shard_map/gather | solution.py:47
  23.2 9.9 %all-to-all-start = ((bf16[128,8,256]{2,1,0:T(8,128)(2,1)}), bf16[128,8,256]{2,1,0:T(8,128)(2,1)}, u32[]{:S(2)}, u32[]{:S(2)}) async-start(bf16[128,8,256]{2,1,0:T(8,128)(2,1)} %bitcast.49), calls=%async_computation | async-start | bytes 1048576 | tf_op jit(solution)/shard_map/all_to_all | solution.py:48
  36.0 10.1 %all-to-all-done = bf16[128,8,256]{2,1,0:T(8,128)(2,1)} async-done(((bf16[128,8,256]{2,1,0:T(8,128)(2,1)}), bf16[128,8,256]{2,1,0:T(8,128)(2,1)}, u32[]{:S(2)}, u32[]{:S(2)}) %all-to-all-start) | async-done | bytes 524320 | tf_op jit(solution)/shard_map/all_to_all | solution.py:48
  46.1 4.8 %all-to-all-start.2 = ((bf16[8,256,256]{2,1,0:T(8,128)(2,1)}), bf16[8,256,256]{2,1,0:T(8,128)(2,1)S(1)}, u32[]{:S(2)}, u32[]{:S(2)}) async-start(bf16[8,256,256]{2,1,0:T(8,128)(2,1)} %bitcast.46), calls=%async_computation.2 | async-start | bytes 2097152 | tf_op jit(solution)/shard_map/all_to_all | solution.py:53
  51.6 14.4 %all-to-all-done.2 = bf16[8,256,256]{2,1,0:T(8,128)(2,1)S(1)} async-done(((bf16[8,256,256]{2,1,0:T(8,128)(2,1)}), bf16[8,256,256]{2,1,0:T(8,128)(2,1)S(1)}, u32[]{:S(2)}, u32[]{:S(2)}) %all-to-all-start.2) | async-done | bytes 1048608 | tf_op jit(solution)/shard_map/all_to_all | solution.py:53
  66.0 10.3 %pad_maximum_fusion = bf16[6144,256]{1,0:T(8,128)(2,1)} fusion(bf16[2048,256]{1,0:T(8,128)(2,1)S(1)} %bitcast.47, bf16[1024,256]{1,0:T(8,128)(2,1)} %bitcast.5, bf16[3072,256]{1,0:T(8,128)(2,1)S(1)} %copy-done.6), kind=kLoop, calls=%fused_computation.43 | loop fusion | flops 9437184 | bytes 6291456 | tf_op jit(solution)/shard_map/concatenate | solution.py:55
  78.2 30.3 %while.20 = (s32[]{:T(128)}, f32[24,128,256]{2,0,1:T(8,128)}, s32[]{:T(128)}, s32[288]{0:T(512)S(1)}, s32[]{:T(128)}, /*index=5*/bf16[288,128,128]{2,1,0:T(8,128...) while((s32[]{:T(128)}, f32[24,128,256]{2,0,1:T(8,128)}, ...), condition=%wide.region_1.2_spmd, body=%wide.region_0.1_spmd.sunk | while | flops 1712068736 | bytes 78650992 | solution.py:81
  79.2 7.9 %gather_fusion = bf16[96,128,256]{2,1,0:T(8,128)(2,1)} fusion(bf16[48,128,256]{2,1,0:T(8,128)(2,1)} %get-tuple-element.264, s32[1024]{0:T(1024)S(1)} %pad_clamp_fusion.5), kind=kCustom, calls=%fused_computation.clone.1 | custom fusion | bytes 12583296 | tf_op jit(solution)/shard_map/while/body/gather | solution.py:72
  87.1 5.7 %fusion.61 = f32[96,128,256]{2,1,0:T(8,128)S(1)} fusion(bf16[96,128,256]{2,1,0:T(8,128)(2,1)} %gather_fusion, bf16[288,128,128]{2,1,0:T(8,128)(2,1)} %get-tuple-element.262, s32[]{:T(128)S(6)} %select_n.56), kind=kOutput, calls=%fused_computation.7.clone.1 | convolution fusion | flops 805306368 | bytes 22020100 | tf_op jit(solution)/shard_map/while/body/tij,tjd->tid/dot_general | solution.py:71
  92.8 13.7 %fusion.62 = f32[24,128,256]{2,0,1:T(8,128)S(1)} fusion(f32[24,128,256]{2,0,1:T(8,128)S(1)} %copy-done.4, f32[96,128,256]{2,1,0:T(8,128)S(1)} %fusion.61, f32[96]{0:T(128)S(1)} %compare_convert_fusion.4, s32[96]{0:T(128)S(1)} %dynamic_slice.32), kind=kOutput, calls=%fused_computation.9.clone.1 | convolution fusion | flops 906760704 | bytes 18875136 | tf_op jit(solution)/shard_map/while/body/tr,tid->rid/dot_general | solution.py:77
  115.5 2.9 fusion.31
  118.5 3.5 broadcast_in_dim.13
  122.0 30.3 %while.21 = (s32[]{:T(128)}, f32[48,128,256]{2,0,1:T(8,128)}, s32[]{:T(128)}, s32[288]{0:T(512)S(1)}, s32[]{:T(128)}, /*index=5*/bf16[288,128,128]{2,1,0:T(8,128...) while((s32[]{:T(128)}, f32[48,128,256]{2,0,1:T(8,128)}, ...), condition=%wide.region_3.4_spmd, body=%wide.region_2.3_spmd.sunk | while | flops 2618829312 | bytes 110108272 | solution.py:117
  122.9 5.9 %gather_fusion.1 = bf16[96,128,256]{2,1,0:T(8,128)(2,1)} fusion(bf16[24,128,256]{2,1,0:T(8,128)(2,1)S(1)} %get-tuple-element.300, s32[1024]{0:T(1024)S(1)} %pad_clamp_fusion.6), kind=kCustom, calls=%fused_computation.1.clone.1 | custom fusion | bytes 12583296 | tf_op jit(solution)/shard_map/while/body/gather | solution.py:108
  128.9 5.7 %fusion.67 = f32[96,128,256]{2,1,0:T(8,128)S(1)} fusion(bf16[96,128,256]{2,1,0:T(8,128)(2,1)} %gather_fusion.1, bf16[288,128,128]{2,1,0:T(8,128)(2,1)} %get-tuple-element.298, s32[]{:T(128)S(6)} %select_n.58), kind=kOutput, calls=%fused_computation.23.clone.1 | convolution fusion | flops 805306368 | bytes 22020100 | tf_op jit(solution)/shard_map/while/body/tji,tjd->tid/dot_general | solution.py:107
  134.6 14.8 %fusion.68 = f32[48,128,256]{2,0,1:T(8,128)S(1)} fusion(f32[48,128,256]{2,0,1:T(8,128)S(1)} %copy-done.2, f32[96,128,256]{2,1,0:T(8,128)S(1)} %fusion.67, f32[96]{0:T(128)S(1)} %compare_convert_fusion.5, s32[96]{0:T(128)S(1)} %dynamic_slice.35), kind=kOutput, calls=%fused_computation.25.clone.1 | convolution fusion | flops 1813521408 | bytes 25166592 | tf_op jit(solution)/shard_map/while/body/tc,tid->cid/dot_general | solution.py:113
  149.4 2.7 copy-done.3
  152.3 6.2 %copy.29 = bf16[48,128,256]{2,1,0:T(8,128)(2,1)S(1)} copy(f32[48,128,256]{2,0,1:T(8,128)} %get-tuple-element.90) | data formatting | bytes 9437184 | tf_op jit(solution)/shard_map/while | solution.py:117
  159.3 123.0 %all-to-all-start.3 = ((bf16[128,8,256]{2,1,0:T(8,128)(2,1)}), bf16[128,8,256]{2,1,0:T(8,128)(2,1)S(1)}, u32[]{:S(2)}, u32[]{:S(2)}) async-start(bf16[128,8,256]{2,1,0:T(8,128)(2,1)} %bitcast.15), calls=%async_computation.3 | async-start | bytes 1048576 | tf_op jit(solution)/shard_map/all_to_all | solution.py:130
  282.4 5.0 %fusion.34 = f32[256,256]{1,0:T(8,128)} fusion(f32[3072,256]{1,0:T(8,128)} %copy-done.7, f32[3072,256]{1,0:T(8,128)} %copy-done.15, bf16[3072,256]{1,0:T(8,128)(2,1)S(1)} %copy-done.11), kind=kOutput, calls=%fused_computation.52 | convolution fusion | flops 411303936 | bytes 8126464 | tf_op jit(solution)/shard_map/dot_general | solution.py:94
  289.6 2.6 copy.28
  292.2 139.4 %all-reduce.2.cloned.1.call-done = f32[256,256]{1,0:T(8,128)} async-done(((f32[256,256]{1,0:T(8,128)}), f32[256,256]{1,0:T(8,128)}) %all-reduce.2.cloned.1.call-update) | async-done | bytes 262160 | tf_op jit(solution)/shard_map/psum | solution.py:133
  433.3 9.7 %scatter_custom_fusion = f32[3072,256]{1,0:T(8,128)} fusion(f32[3072,256]{1,0:T(8,128)} %bitcast.48, s32[1024]{0:T(1024)} %bitcast.51, bf16[128,8,256]{2,1,0:T(8,128)(2,1)S(1)} %all-to-all-done.3), kind=kCustom, calls=%fused_computation.50 | custom fusion | flops 524288 | bytes 3670016 | tf_op jit(solution)/shard_map/scatter-add | solution.py:132
  (62 shorter events, 22.7 us)
Async XLA Ops:
  7.2 27.2 %copy-start = (bf16[3072,256]{1,0:T(8,128)(2,1)S(1)}, bf16[3072,256]{1,0:T(8,128)(2,1)}, u32[]{:S(2)}) copy-start(bf16[3072,256]{1,0:T(8,128)(2,1)} %param.17) | copy-start | bytes 4718596
  8.6 14.5 %all-to-all-start.1 = ((s32[8,1,2]{2,1,0:T(1,128)}), s32[8,1,2]{2,1,0:T(1,128)S(1)}, u32[]{:S(2)}, u32[]{:S(2)}) async-start(s32[8,1,2]{2,1,0:T(1,128)} %copy.25), calls=%async_computation.1 | async-start | bytes 8192 | tf_op jit(solution)/shard_map/all_to_all | solution.py:50
  16.4 0.6 copy-start.9
  23.2 42.9 %copy-start.6 = (bf16[3072,256]{1,0:T(8,128)(2,1)S(1)}, bf16[3072,256]{1,0:T(8,128)(2,1)}, u32[]{:S(2)}) copy-start(bf16[3072,256]{1,0:T(8,128)(2,1)} %param.15) | copy-start | bytes 4718596
  23.2 22.9 %all-to-all-start = ((bf16[128,8,256]{2,1,0:T(8,128)(2,1)}), bf16[128,8,256]{2,1,0:T(8,128)(2,1)}, u32[]{:S(2)}, u32[]{:S(2)}) async-start(bf16[128,8,256]{2,1,0:T(8,128)(2,1)} %bitcast.49), calls=%async_computation | async-start | bytes 1048576 | tf_op jit(solution)/shard_map/all_to_all | solution.py:48
  46.1 19.9 %all-to-all-start.2 = ((bf16[8,256,256]{2,1,0:T(8,128)(2,1)}), bf16[8,256,256]{2,1,0:T(8,128)(2,1)S(1)}, u32[]{:S(2)}, u32[]{:S(2)}) async-start(bf16[8,256,256]{2,1,0:T(8,128)(2,1)} %bitcast.46), calls=%async_computation.2 | async-start | bytes 2097152 | tf_op jit(solution)/shard_map/all_to_all | solution.py:53
  76.3 1.9 copy-start.13
  76.3 1.9 copy-start.14
  87.1 5.7 %copy-start.4 = (f32[24,128,256]{2,0,1:T(8,128)S(1)}, f32[24,128,256]{2,0,1:T(8,128)}, u32[]{:S(2)}) copy-start(f32[24,128,256]{2,0,1:T(8,128)} %get-tuple-element.246) | copy-start | bytes 9437188 | tf_op jit(solution)/shard_map/while
  106.5 1.7 copy-start.5
  110.7 1.4 copy-start.8
  112.1 0.9 copy-start.12
  113.0 2.3 copy-start.7
  113.0 2.5 copy-start.10
  115.3 3.2 copy-start.15
  128.9 5.7 %copy-start.2 = (f32[48,128,256]{2,0,1:T(8,128)S(1)}, f32[48,128,256]{2,0,1:T(8,128)}, u32[]{:S(2)}) copy-start(f32[48,128,256]{2,0,1:T(8,128)} %get-tuple-element.282) | copy-start | bytes 18874372 | tf_op jit(solution)/shard_map/while
  149.4 2.7 copy-start.3
  152.2 130.1 %copy-start.11 = (bf16[3072,256]{1,0:T(8,128)(2,1)S(1)}, bf16[3072,256]{1,0:T(8,128)(2,1)}, u32[]{:S(2)}) copy-start(bf16[3072,256]{1,0:T(8,128)(2,1)} %param.18) | copy-start | bytes 4718596
  159.3 273.9 %all-to-all-start.3 = ((bf16[128,8,256]{2,1,0:T(8,128)(2,1)}), bf16[128,8,256]{2,1,0:T(8,128)(2,1)S(1)}, u32[]{:S(2)}, u32[]{:S(2)}) async-start(bf16[128,8,256]{2,1,0:T(8,128)(2,1)} %bitcast.15), calls=%async_computation.3 | async-start | bytes 1048576 | tf_op jit(solution)/shard_map/all_to_all | solution.py:130
  282.3 149.3 %all-reduce.2.cloned.1.call-start = ((), (), s32[]{:S(2)}) async-start(), calls=%async_computation.4 | async-start | bytes 524288 | tf_op jit(solution)/shard_map/psum | solution.py:133
  289.5 153.5 %copy-start.1 = (bf16[3072,256]{1,0:T(8,128)(2,1)S(1)}, bf16[3072,256]{1,0:T(8,128)(2,1)}, u32[]{:S(2)}) copy-start(bf16[3072,256]{1,0:T(8,128)(2,1)} %param.17) | copy-start | bytes 4718596
Sparse Core Ops, SparseCore 0:
  288.5 143.0 all-reduce.1
where the time goes:
time: 456 us; the launch traced here: 450 us
  waiting for transfers between devices  164 us (36%)
  starting transfers between devices  145 us (32%)
  matrix products  50.1 us (11%)
  local copies, waits for them, and re-layouts  48.9 us (11%)
  other arithmetic  26.4 us (6%)
  between operations  15.1 us (3%)
    psum x1, waiting for transfers between devices, per_device(): weight_total = lax.psum(weight_part, ('dom', 'grp'))  139 us
    all_to_all x1, starting transfers between devices, per_device(): lax.all_to_all(fresh_grads, ('dom', 'grp'), split_axis=0, concat_axis=0,...  123 us
    dot_general x1, matrix products, backward_turn(): jnp.einsum('tc,tid->cid', onto_mask, spread, precision=lax.Precision.HIGH...  14.8 us
    all_to_all x1, waiting for transfers between devices, per_device(): lax.all_to_all(served, 'dom', split_axis=0, concat_axis=0, tiled=True)  14.4 us
    dot_general x1, matrix products, forward_turn(): jnp.einsum('tr,tid->rid', placing, products, precision=lax.Precision.HIGH...  13.7 us
    concatenate x1, other arithmetic, per_device(): columns = jnp.concatenate([inputs, arrived, cached], axis=0)  10.3 us
    all_to_all x1, waiting for transfers between devices, per_device(): lax.all_to_all(outgoing, ('dom', 'grp'), split_axis=0, concat_axis=0, til...  10.1 us
    all_to_all x1, starting transfers between devices, per_device(): lax.all_to_all(outgoing, ('dom', 'grp'), split_axis=0, concat_axis=0, til...  9.95 us
  transfers between devices with their start and end apart: 5, of which 3 were waited for; matrix products, arithmetic and copies ran while one was open for 5% of the time, Pallas kernels for 0%

commit v1 on v0

--- a/solution.py
+++ b/solution.py
@@ -130,7 +130,9 @@
     returned = lax.all_to_all(fresh_grads, ("dom", "grp"), split_axis=0, concat_axis=0, tiled=True)
     returned = returned.reshape(peer_count * per_peer, feature_dim).astype(jnp.float32)
     grad_inputs = own_grads.at[send_list.reshape(-1)].add(returned)
-    weight_total = lax.psum(weight_part, ("dom", "grp"))
+    weight_total = weight_part
+    for name in ("dom", "grp"):
+        weight_total = lax.psum(weight_total, name)
     grad_weight = weight_total * (beta_map / math.sqrt(row_count * peer_count))
     return (layer_out, grad_inputs, grad_weight)
 

time: 456 us -> 402 us (0.88)
  waiting for transfers between devices: 164 us -> 108 us
    psum x1 -> x2, waiting for transfers between devices: 139 us -> 83 us  [per_device(): weight_total = lax.psum(weight_total, name)]
  transfers between devices with their start and end apart: 5 -> 6, of which waited for: 3 -> 3; matrix products, arithmetic and copies ran while one was open for 5% -> 14% of each run, Pallas kernels for 0% -> 0%
where the time goes in v1:
time: 402 us; the launch traced here: 396 us
  starting transfers between devices  145 us (36%)
  waiting for transfers between devices  108 us (27%)
  local copies, waits for them, and re-layouts  50.3 us (13%)
  matrix products  49.9 us (12%)
  other arithmetic  26.4 us (7%)
  between operations  15.1 us (4%)
    all_to_all x1, starting transfers between devices, per_device(): lax.all_to_all(fresh_grads, ('dom', 'grp'), split_axis=0, concat_axis=0,...  123 us
    psum x2, waiting for transfers between devices, per_device(): weight_total = lax.psum(weight_total, name)  83 us
    dot_general x1, matrix products, backward_turn(): jnp.einsum('tc,tid->cid', onto_mask, spread, precision=lax.Precision.HIGH...  14.8 us
    all_to_all x1, waiting for transfers between devices, per_device(): lax.all_to_all(served, 'dom', split_axis=0, concat_axis=0, tiled=True)  14.4 us
    dot_general x1, matrix products, forward_turn(): jnp.einsum('tr,tid->rid', placing, products, precision=lax.Precision.HIGH...  13.7 us
    concatenate x1, other arithmetic, per_device(): columns = jnp.concatenate([inputs, arrived, cached], axis=0)  10.3 us
    all_to_all x1, waiting for transfers between devices, per_device(): lax.all_to_all(outgoing, ('dom', 'grp'), split_axis=0, concat_axis=0, til...  10.1 us
    all_to_all x1, starting transfers between devices, per_device(): lax.all_to_all(outgoing, ('dom', 'grp'), split_axis=0, concat_axis=0, til...  9.95 us
  transfers between devices with their start and end apart: 6, of which 3 were waited for; matrix products, arithmetic and copies ran while one was open for 14% of the time, Pallas kernels for 0%

profile of v1, /device:TPU:1, one launch (start us, length us, event | category | flops | bytes accessed | tf_op | source)
XLA Modules:
  0.0 395.8 jit_solution(10505469015950495526)
XLA Ops:
  8.6 6.8 %all-to-all-start.1 = ((s32[8,1,2]{2,1,0:T(1,128)}), s32[8,1,2]{2,1,0:T(1,128)S(1)}, u32[]{:S(2)}, u32[]{:S(2)}) async-start(s32[8,1,2]{2,1,0:T(1,128)} %copy.25), calls=%async_computation.1 | async-start | bytes 8192 | tf_op jit(solution)/shard_map/all_to_all | solution.py:50
  17.0 6.2 %gather_fusion.2 = bf16[1024,256]{1,0:T(8,128)(2,1)} fusion(bf16[3072,256]{1,0:T(8,128)(2,1)} %param.15, s32[1024]{0:T(1024)S(1)} %broadcast_clamp_fusion), kind=kCustom, calls=%fused_computation.2 | custom fusion | bytes 1052672 | tf_op jit(solution)/shard_map/gather | solution.py:47
  23.2 9.9 %all-to-all-start = ((bf16[128,8,256]{2,1,0:T(8,128)(2,1)}), bf16[128,8,256]{2,1,0:T(8,128)(2,1)}, u32[]{:S(2)}, u32[]{:S(2)}) async-start(bf16[128,8,256]{2,1,0:T(8,128)(2,1)} %bitcast.49), calls=%async_computation | async-start | bytes 1048576 | tf_op jit(solution)/shard_map/all_to_all | solution.py:48
  36.0 10.1 %all-to-all-done = bf16[128,8,256]{2,1,0:T(8,128)(2,1)} async-done(((bf16[128,8,256]{2,1,0:T(8,128)(2,1)}), bf16[128,8,256]{2,1,0:T(8,128)(2,1)}, u32[]{:S(2)}, u32[]{:S(2)}) %all-to-all-start) | async-done | bytes 524320 | tf_op jit(solution)/shard_map/all_to_all | solution.py:48
  46.1 4.8 %all-to-all-start.2 = ((bf16[8,256,256]{2,1,0:T(8,128)(2,1)}), bf16[8,256,256]{2,1,0:T(8,128)(2,1)S(1)}, u32[]{:S(2)}, u32[]{:S(2)}) async-start(bf16[8,256,256]{2,1,0:T(8,128)(2,1)} %bitcast.46), calls=%async_computation.2 | async-start | bytes 2097152 | tf_op jit(solution)/shard_map/all_to_all | solution.py:53
  51.6 14.4 %all-to-all-done.2 = bf16[8,256,256]{2,1,0:T(8,128)(2,1)S(1)} async-done(((bf16[8,256,256]{2,1,0:T(8,128)(2,1)}), bf16[8,256,256]{2,1,0:T(8,128)(2,1)S(1)}, u32[]{:S(2)}, u32[]{:S(2)}) %all-to-all-start.2) | async-done | bytes 1048608 | tf_op jit(solution)/shard_map/all_to_all | solution.py:53
  66.0 10.3 %pad_maximum_fusion = bf16[6144,256]{1,0:T(8,128)(2,1)} fusion(bf16[2048,256]{1,0:T(8,128)(2,1)S(1)} %bitcast.47, bf16[1024,256]{1,0:T(8,128)(2,1)} %bitcast.5, bf16[3072,256]{1,0:T(8,128)(2,1)S(1)} %copy-done.6), kind=kLoop, calls=%fused_computation.43 | loop fusion | flops 9437184 | bytes 6291456 | tf_op jit(solution)/shard_map/concatenate | solution.py:55
  78.2 30.3 %while.20 = (s32[]{:T(128)}, f32[24,128,256]{2,0,1:T(8,128)}, s32[]{:T(128)}, s32[288]{0:T(512)S(1)}, s32[]{:T(128)}, /*index=5*/bf16[288,128,128]{2,1,0:T(8,128...) while((s32[]{:T(128)}, f32[24,128,256]{2,0,1:T(8,128)}, ...), condition=%wide.region_1.2_spmd, body=%wide.region_0.1_spmd.sunk | while | flops 1712068736 | bytes 78650992 | solution.py:81
  79.2 7.9 %gather_fusion = bf16[96,128,256]{2,1,0:T(8,128)(2,1)} fusion(bf16[48,128,256]{2,1,0:T(8,128)(2,1)} %get-tuple-element.264, s32[1024]{0:T(1024)S(1)} %pad_clamp_fusion.5), kind=kCustom, calls=%fused_computation.clone.1 | custom fusion | bytes 12583296 | tf_op jit(solution)/shard_map/while/body/gather | solution.py:72
  87.1 5.7 %fusion.61 = f32[96,128,256]{2,1,0:T(8,128)S(1)} fusion(bf16[96,128,256]{2,1,0:T(8,128)(2,1)} %gather_fusion, bf16[288,128,128]{2,1,0:T(8,128)(2,1)} %get-tuple-element.262, s32[]{:T(128)S(6)} %select_n.56), kind=kOutput, calls=%fused_computation.7.clone.1 | convolution fusion | flops 805306368 | bytes 22020100 | tf_op jit(solution)/shard_map/while/body/tij,tjd->tid/dot_general | solution.py:71
  92.8 13.7 %fusion.62 = f32[24,128,256]{2,0,1:T(8,128)S(1)} fusion(f32[24,128,256]{2,0,1:T(8,128)S(1)} %copy-done.4, f32[96,128,256]{2,1,0:T(8,128)S(1)} %fusion.61, f32[96]{0:T(128)S(1)} %compare_convert_fusion.4, s32[96]{0:T(128)S(1)} %dynamic_slice.32), kind=kOutput, calls=%fused_computation.9.clone.1 | convolution fusion | flops 906760704 | bytes 18875136 | tf_op jit(solution)/shard_map/while/body/tr,tid->rid/dot_general | solution.py:77
  113.0 2.3 multiply_convert_fusion
  119.2 5.6 %fusion.31 = bf16[3072,256]{1,0:T(8,128)(2,1)S(1)} fusion(bf16[256,256]{1,0:T(8,128)(2,1)S(1)} %copy-done.10, f32[3072,256]{1,0:T(8,128)} %copy-done.13, bf16[3072,256]{1,0:T(8,128)(2,1)S(1)} %copy-done.9), kind=kOutput, calls=%fused_computation.42 | convolution fusion | flops 421527552 | bytes 6422528 | tf_op jit(solution)/shard_map/dot_general | solution.py:97
  124.8 3.5 broadcast_in_dim.13
  128.3 30.3 %while.21 = (s32[]{:T(128)}, f32[48,128,256]{2,0,1:T(8,128)}, s32[]{:T(128)}, s32[288]{0:T(512)S(1)}, s32[]{:T(128)}, /*index=5*/bf16[288,128,128]{2,1,0:T(8,128...) while((s32[]{:T(128)}, f32[48,128,256]{2,0,1:T(8,128)}, ...), condition=%wide.region_3.4_spmd, body=%wide.region_2.3_spmd.sunk | while | flops 2618829312 | bytes 110108272 | solution.py:117
  129.3 6.0 %gather_fusion.1 = bf16[96,128,256]{2,1,0:T(8,128)(2,1)} fusion(bf16[24,128,256]{2,1,0:T(8,128)(2,1)S(1)} %get-tuple-element.300, s32[1024]{0:T(1024)S(1)} %pad_clamp_fusion.6), kind=kCustom, calls=%fused_computation.1.clone.1 | custom fusion | bytes 12583296 | tf_op jit(solution)/shard_map/while/body/gather | solution.py:108
  135.2 5.7 %fusion.67 = f32[96,128,256]{2,1,0:T(8,128)S(1)} fusion(bf16[96,128,256]{2,1,0:T(8,128)(2,1)} %gather_fusion.1, bf16[288,128,128]{2,1,0:T(8,128)(2,1)} %get-tuple-element.298, s32[]{:T(128)S(6)} %select_n.58), kind=kOutput, calls=%fused_computation.23.clone.1 | convolution fusion | flops 805306368 | bytes 22020100 | tf_op jit(solution)/shard_map/while/body/tji,tjd->tid/dot_general | solution.py:107
  141.0 14.8 %fusion.68 = f32[48,128,256]{2,0,1:T(8,128)S(1)} fusion(f32[48,128,256]{2,0,1:T(8,128)S(1)} %copy-done.2, f32[96,128,256]{2,1,0:T(8,128)S(1)} %fusion.67, f32[96]{0:T(128)S(1)} %compare_convert_fusion.5, s32[96]{0:T(128)S(1)} %dynamic_slice.35), kind=kOutput, calls=%fused_computation.25.clone.1 | convolution fusion | flops 1813521408 | bytes 25166592 | tf_op jit(solution)/shard_map/while/body/tc,tid->cid/dot_general | solution.py:113
  155.8 2.7 copy-done.3
  158.6 6.1 %copy.29 = bf16[48,128,256]{2,1,0:T(8,128)(2,1)S(1)} copy(f32[48,128,256]{2,0,1:T(8,128)} %get-tuple-element.90) | data formatting | bytes 9437184 | tf_op jit(solution)/shard_map/while | solution.py:117
  165.6 123.2 %all-to-all-start.3 = ((bf16[128,8,256]{2,1,0:T(8,128)(2,1)}), bf16[128,8,256]{2,1,0:T(8,128)(2,1)S(1)}, u32[]{:S(2)}, u32[]{:S(2)}) async-start(bf16[128,8,256]{2,1,0:T(8,128)(2,1)} %bitcast.15), calls=%async_computation.3 | async-start | bytes 1048576 | tf_op jit(solution)/shard_map/all_to_all | solution.py:130
  291.6 2.6 copy.28
  294.3 83.0 %all-reduce.5.cloned.1.call-done = f32[256,256]{1,0:T(8,128)} async-done(((f32[256,256]{1,0:T(8,128)}), f32[256,256]{1,0:T(8,128)}) %all-reduce.5.cloned.1.call-update) | async-done | bytes 262160 | tf_op jit(solution)/shard_map/psum | solution.py:135
  378.9 9.7 %scatter_custom_fusion = f32[3072,256]{1,0:T(8,128)} fusion(f32[3072,256]{1,0:T(8,128)} %bitcast.48, s32[1024]{0:T(1024)} %bitcast.51, bf16[128,8,256]{2,1,0:T(8,128)(2,1)S(1)} %all-to-all-done.3), kind=kCustom, calls=%fused_computation.50 | custom fusion | flops 524288 | bytes 3670016 | tf_op jit(solution)/shard_map/scatter-add | solution.py:132
  (61 shorter events, 24.7 us)
Async XLA Ops:
  7.2 27.2 %copy-start = (bf16[3072,256]{1,0:T(8,128)(2,1)S(1)}, bf16[3072,256]{1,0:T(8,128)(2,1)}, u32[]{:S(2)}) copy-start(bf16[3072,256]{1,0:T(8,128)(2,1)} %param.17) | copy-start | bytes 4718596
  8.6 14.5 %all-to-all-start.1 = ((s32[8,1,2]{2,1,0:T(1,128)}), s32[8,1,2]{2,1,0:T(1,128)S(1)}, u32[]{:S(2)}, u32[]{:S(2)}) async-start(s32[8,1,2]{2,1,0:T(1,128)} %copy.25), calls=%async_computation.1 | async-start | bytes 8192 | tf_op jit(solution)/shard_map/all_to_all | solution.py:50
  16.4 0.6 copy-start.8
  23.2 42.9 %copy-start.6 = (bf16[3072,256]{1,0:T(8,128)(2,1)S(1)}, bf16[3072,256]{1,0:T(8,128)(2,1)}, u32[]{:S(2)}) copy-start(bf16[3072,256]{1,0:T(8,128)(2,1)} %param.15) | copy-start | bytes 4718596
  23.2 22.9 %all-to-all-start = ((bf16[128,8,256]{2,1,0:T(8,128)(2,1)}), bf16[128,8,256]{2,1,0:T(8,128)(2,1)}, u32[]{:S(2)}, u32[]{:S(2)}) async-start(bf16[128,8,256]{2,1,0:T(8,128)(2,1)} %bitcast.49), calls=%async_computation | async-start | bytes 1048576 | tf_op jit(solution)/shard_map/all_to_all | solution.py:48
  46.1 19.9 %all-to-all-start.2 = ((bf16[8,256,256]{2,1,0:T(8,128)(2,1)}), bf16[8,256,256]{2,1,0:T(8,128)(2,1)S(1)}, u32[]{:S(2)}, u32[]{:S(2)}) async-start(bf16[8,256,256]{2,1,0:T(8,128)(2,1)} %bitcast.46), calls=%async_computation.2 | async-start | bytes 2097152 | tf_op jit(solution)/shard_map/all_to_all | solution.py:53
  50.9 237.9 %all-reduce.3.cloned.1.call-start = ((), (), s32[]{:S(2)}) async-start(), calls=%async_computation.4 | async-start | bytes 524288 | tf_op jit(solution)/shard_map/psum | solution.py:135
  76.3 1.9 copy-start.11
  76.3 1.9 copy-start.12
  87.1 5.7 %copy-start.4 = (f32[24,128,256]{2,0,1:T(8,128)S(1)}, f32[24,128,256]{2,0,1:T(8,128)}, u32[]{:S(2)}) copy-start(f32[24,128,256]{2,0,1:T(8,128)} %get-tuple-element.246) | copy-start | bytes 9437188 | tf_op jit(solution)/shard_map/while
  106.5 1.7 copy-start.5
  110.7 1.4 copy-start.7
  112.1 0.9 copy-start.10
  113.0 4.0 %copy-start.9 = (bf16[3072,256]{1,0:T(8,128)(2,1)S(1)}, bf16[3072,256]{1,0:T(8,128)(2,1)}, u32[]{:S(2)}) copy-start(bf16[3072,256]{1,0:T(8,128)(2,1)} %param.18) | copy-start | bytes 4718596
  115.3 1.7 copy-start.13
  135.2 5.7 %copy-start.2 = (f32[48,128,256]{2,0,1:T(8,128)S(1)}, f32[48,128,256]{2,0,1:T(8,128)}, u32[]{:S(2)}) copy-start(f32[48,128,256]{2,0,1:T(8,128)} %get-tuple-element.282) | copy-start | bytes 18874372 | tf_op jit(solution)/shard_map/while
  155.8 2.7 copy-start.3
  165.6 213.4 %all-to-all-start.3 = ((bf16[128,8,256]{2,1,0:T(8,128)(2,1)}), bf16[128,8,256]{2,1,0:T(8,128)(2,1)S(1)}, u32[]{:S(2)}, u32[]{:S(2)}) async-start(bf16[128,8,256]{2,1,0:T(8,128)(2,1)} %bitcast.15), calls=%async_computation.3 | async-start | bytes 1048576 | tf_op jit(solution)/shard_map/all_to_all | solution.py:130
  288.7 88.5 %all-reduce.5.cloned.1.call-start = ((), (), s32[]{:S(2)}) async-start(), calls=%async_computation.5 | async-start | bytes 524288 | tf_op jit(solution)/shard_map/psum | solution.py:135
  291.6 97.1 %copy-start.1 = (bf16[3072,256]{1,0:T(8,128)(2,1)S(1)}, bf16[3072,256]{1,0:T(8,128)(2,1)}, u32[]{:S(2)}) copy-start(bf16[3072,256]{1,0:T(8,128)(2,1)} %param.17) | copy-start | bytes 4718596
Sparse Core Ops, SparseCore 0:
  125.0 112.8 all-reduce.2
  293.1 84.1 all-reduce.4
